TPU v7x, 32 devices: a whole 2x2x4 slice. The times are simulated.
32 devices in a mesh: blk: 2 (over x), theta: 4 (over z), radial: 4 (over y, core).
Axes of the slice: x: 2, y: 2, z: 4, core: 2. Of those that a mesh axis runs over, the one named last changes fastest.
Arguments:
- base_state: float32 [5, 12, 32, 4096], P(None, 'blk', 'radial', 'theta'), may hold values from -4 to 12, as said below
- section_state: float32 [5, 12, 32, 4096], P(None, 'blk', 'radial', 'theta'), may hold values from -4 to 12, as said below
- rotor_step: int32 [1], replicated, may hold values from 4096 to 16383
Outputs:
- next_state: float32 [5, 12, 32, 4096], P(None, 'blk', 'radial', 'theta')
Inputs may be any that keep to these rules, and one draw needn't show every extreme that they name: `base_state`: density between 0.5 and 2, pressure between 0.5 and 2, every velocity component under 2 in magnitude. `section_state`: density between 0.5 and 2, pressure between 0.5 and 2, every velocity component under 2 in magnitude.
All inputs are finite; a program needn't handle non-finite values.
Results may differ from a plain program's by a relative error of at most 0.0003.
Values sent between devices are 32-bit elements; how exact they have to be, the bound alone decides.
No kernel may reach another device: no remote copies, remote signals or barrier semaphores. Data moves between devices by JAX's collectives and lax.ppermute only.
A program may use at most 64 MiB of HBM per device.

v0:
```python
import jax
import jax.numpy as jnp
from jax import lax
from jax.sharding import PartitionSpec as P

gamma_ratio = 1.4
weno_epsilon = 1e-06
step_ratio = 0.12


def padded_2(cells, sides, width, closed):
    for axis, dim in sides:
        count = lax.axis_size(axis)
        ends = count if closed else count - 1
        head = lax.slice_in_dim(cells, 0, width, axis=dim)
        tail = lax.slice_in_dim(cells, cells.shape[dim] - width, cells.shape[dim], axis=dim)
        cells = jnp.concatenate(
            [
                lax.ppermute(tail, axis, [(i, (i + 1) % count) for i in range(ends)]),
                cells,
                lax.ppermute(head, axis, [((i + 1) % count, i) for i in range(ends)]),
            ],
            axis=dim,
        )
    return cells


def partner(block, axis, distance):
    count = lax.axis_size(axis)
    route = []
    for low in range(count):
        high = low | 1 << distance
        if high != low and high < count:
            route += [(low, high), (high, low)]
    return lax.ppermute(block, axis, route)


def pressure_of(state):
    kinetic = 0.5 * (jnp.square(state[1]) + jnp.square(state[2]) + jnp.square(state[3])) / state[0]
    return (gamma_ratio - 1.0) * (state[4] - kinetic)


def euler_flux(state, normal):
    pressure = pressure_of(state)
    velocity = state[normal] / state[0]
    flux = state * velocity[None]
    flux = flux.at[normal].add(pressure)
    flux = flux.at[4].add(pressure * velocity)
    return flux


def wave_speed(state, normal):
    pressure = pressure_of(state)
    return jnp.abs(state[normal] / state[0]) + jnp.sqrt(gamma_ratio * pressure / state[0])


def weno_side(far_left, left_cell, centre, right_cell, far_right):
    smooth_low = 13.0 / 12.0 * jnp.square(far_left - 2.0 * left_cell + centre) + 0.25 * jnp.square(
        far_left - 4.0 * left_cell + 3.0 * centre
    )
    smooth_mid = 13.0 / 12.0 * jnp.square(
        left_cell - 2.0 * centre + right_cell
    ) + 0.25 * jnp.square(left_cell - right_cell)
    smooth_high = 13.0 / 12.0 * jnp.square(
        centre - 2.0 * right_cell + far_right
    ) + 0.25 * jnp.square(3.0 * centre - 4.0 * right_cell + far_right)
    weight_low = 0.1 / jnp.square(weno_epsilon + smooth_low)
    weight_mid = 0.6 / jnp.square(weno_epsilon + smooth_mid)
    weight_high = 0.3 / jnp.square(weno_epsilon + smooth_high)
    guess_low = (2.0 * far_left - 7.0 * left_cell + 11.0 * centre) / 6.0
    guess_mid = (-left_cell + 5.0 * centre + 2.0 * right_cell) / 6.0
    guess_high = (2.0 * centre + 5.0 * right_cell - far_right) / 6.0
    return (weight_low * guess_low + weight_mid * guess_mid + weight_high * guess_high) / (
        weight_low + weight_mid + weight_high
    )


def face_flux(padded, fluxes, axis, count, normal, first, second):
    states = [
        lax.slice_in_dim(padded, shift_index, shift_index + count + 1, axis=axis)
        for shift_index in range(6)
    ]
    physical = [
        lax.slice_in_dim(fluxes, shift_index, shift_index + count + 1, axis=axis)
        for shift_index in range(6)
    ]
    mean = 0.5 * (states[2] + states[3])
    density = mean[0]
    normal_speed = mean[normal] / density
    speed_first = mean[first] / density
    speed_second = mean[second] / density
    kinetic = 0.5 * (jnp.square(normal_speed) + jnp.square(speed_first) + jnp.square(speed_second))
    pressure = pressure_of(mean)
    sound = jnp.sqrt(gamma_ratio * pressure / density)
    enthalpy = (mean[4] + pressure) / density
    inv_sound = 1.0 / sound
    factor_one = (gamma_ratio - 1.0) * jnp.square(inv_sound)
    factor_two = factor_one * kinetic
    dissipation = jnp.maximum(wave_speed(states[2], normal), wave_speed(states[3], normal))

    def project(vector):
        dens_part = vector[0]
        norm_part = vector[normal]
        first_part = vector[first]
        second_part = vector[second]
        energy_part = vector[4]
        tangent_sum = factor_one * (
            speed_first * first_part + speed_second * second_part - energy_part
        )
        wave_minus = 0.5 * (
            (factor_two + normal_speed * inv_sound) * dens_part
            - (factor_one * normal_speed + inv_sound) * norm_part
            - tangent_sum
        )
        entropy = (
            (1.0 - factor_two) * dens_part + factor_one * normal_speed * norm_part + tangent_sum
        )
        shear_first = first_part - speed_first * dens_part
        shear_second = second_part - speed_second * dens_part
        wave_plus = 0.5 * (
            (factor_two - normal_speed * inv_sound) * dens_part
            - (factor_one * normal_speed - inv_sound) * norm_part
            - tangent_sum
        )
        return (wave_minus, entropy, shear_first, shear_second, wave_plus)

    state_chars = [project(cell_state) for cell_state in states]
    flux_chars = [project(cell_flux) for cell_flux in physical]
    recon = []
    for field_index in range(5):
        plus_vals = [
            0.5 * (flux_chars[cell][field_index] + dissipation * state_chars[cell][field_index])
            for cell in range(6)
        ]
        minus_vals = [
            0.5 * (flux_chars[cell][field_index] - dissipation * state_chars[cell][field_index])
            for cell in range(6)
        ]
        recon.append(
            weno_side(plus_vals[0], plus_vals[1], plus_vals[2], plus_vals[3], plus_vals[4])
            + weno_side(minus_vals[5], minus_vals[4], minus_vals[3], minus_vals[2], minus_vals[1])
        )
    wave_minus, entropy, shear_first, shear_second, wave_plus = recon
    acoustic = wave_minus + entropy + wave_plus
    parts = {}
    parts[0] = acoustic
    parts[normal] = (
        (normal_speed - sound) * wave_minus
        + normal_speed * entropy
        + (normal_speed + sound) * wave_plus
    )
    parts[first] = speed_first * acoustic + shear_first
    parts[second] = speed_second * acoustic + shear_second
    parts[4] = (
        (enthalpy - normal_speed * sound) * wave_minus
        + kinetic * entropy
        + speed_first * shear_first
        + speed_second * shear_second
        + (enthalpy + normal_speed * sound) * wave_plus
    )
    return jnp.stack([parts[index_part] for index_part in range(5)])


def divergence(padded, axis, count, normal, first, second):
    faces = face_flux(padded, euler_flux(padded, normal), axis, count, normal, first, second)
    return lax.slice_in_dim(faces, 1, count + 1, axis=axis) - lax.slice_in_dim(
        faces, 0, count, axis=axis
    )


def flip_radial(cells):
    turned = cells[:, :, ::-1]
    return jnp.concatenate([turned[:3], -turned[3:4], turned[4:]], axis=0)


def flip_theta(cells):
    return jnp.concatenate([cells[:2], -cells[2:3], cells[3:]], axis=0)


def shards(base_state, section_state, rotor_step):
    planes = section_state.shape[1]
    bands = section_state.shape[2]
    width = section_state.shape[3]
    offset = rotor_step[0] // 4
    fraction = (rotor_step[0] % 4).astype(jnp.float32) / 4.0
    theta_padded = padded_2(section_state, (("theta", 3),), 3, True)
    radial_raw = padded_2(section_state, (("radial", 2),), 3, False)
    band_index = lax.axis_index("radial")
    band_count = lax.axis_size("radial")
    lower_wall = jnp.where(
        band_index == 0, flip_radial(section_state[:, :, :3]), radial_raw[:, :, :3]
    )
    upper_wall = jnp.where(
        band_index == band_count - 1, flip_radial(section_state[:, :, -3:]), radial_raw[:, :, -3:]
    )
    radial_padded = jnp.concatenate([lower_wall, section_state, upper_wall], axis=2)
    block_index = lax.axis_index("blk")
    outgoing = jnp.where(block_index == 0, section_state[:, -3:], section_state[:, :3])
    slab_count = lax.axis_size("theta")
    slab_index = lax.axis_index("theta")
    turns = offset // width
    facing = partner(outgoing, "blk", 0)
    whole = lax.all_gather(facing, "theta", axis=3, tiled=True)
    doubled = jnp.concatenate([whole, whole], axis=3)
    start = (turns - 1 - slab_index) % slab_count * width
    window = lax.dynamic_slice_in_dim(doubled, start, 2 * width, 3)
    reversed_window = window[..., ::-1]
    remainder = offset % width
    low_part = lax.dynamic_slice_in_dim(reversed_window, width - remainder, width, 3)
    high_part = lax.dynamic_slice_in_dim(reversed_window, width - remainder - 1, width, 3)
    ghost = flip_theta((1.0 - fraction) * low_part + fraction * high_part)
    edge_low = jnp.concatenate(
        [section_state[:, :1], section_state[:, :1], section_state[:, :1]], axis=1
    )
    edge_high = jnp.concatenate(
        [section_state[:, -1:], section_state[:, -1:], section_state[:, -1:]], axis=1
    )
    lower_axial = jnp.where(block_index == 0, edge_low, ghost)
    upper_axial = jnp.where(block_index == 0, ghost, edge_high)
    axial_padded = jnp.concatenate([lower_axial, section_state, upper_axial], axis=1)
    axial = divergence(axial_padded, 1, planes, 1, 2, 3)
    radial = divergence(radial_padded, 2, bands, 3, 1, 2)
    azimuthal = divergence(theta_padded, 3, width, 2, 1, 3)
    change = -step_ratio * (axial + radial + azimuthal)
    return 0.75 * base_state + 0.25 * (section_state + change)


def solution(mesh):
    in_specs = (P(None, "blk", "radial", "theta"), P(None, "blk", "radial", "theta"), P())
    out_specs = P(None, "blk", "radial", "theta")
    return jax.shard_map(shards, mesh=mesh, in_specs=in_specs, out_specs=out_specs, check_vma=False)
```

profile of v0, /device:TPU:1, one launch (start us, length us, event | category | flops | bytes accessed | tf_op | source)
XLA Modules:
  0.0 161.8 jit_solution(2195187401724446595)
XLA Ops:
  6.5 1.8 %fusion.400 = (f32[5,6,8,1024]{3,1,2,0:T(8,128)S(1)}, f32[5,6,8,1027]{3,1,2,0:T(8,128)S(1)}) fusion(f32[5,6,8,1024]{3,2,1,0:T(8,128)} %param.16), kind=kLoop, calls=%fused_computation.748 | loop fusion | bytes 3604480 | tf_op args[1]
  8.4 0.8 fusion.399
  9.2 4.2 %collective-permute-start.4 = (f32[5,6,8,3]{3,1,2,0:T(8,128)}, f32[5,6,8,3]{3,1,2,0:T(8,128)}, u32[]{:S(2)}, u32[]{:S(2)}) collective-permute-start(f32[5,6,8,3]{3,1,2,0:T(8,128)} %get-tuple-element.206), channel_id=1, source_target_pairs={{4,0},{8,4},{12,8},{0,12},{5,1},{9,5},{13,9},{1,13},{6,2},{10,6},{... | collective-permute-start | bytes 8648 | tf_op jit(solution)/shard_map/ppermute | solution.py:21
  13.3 1.0 fusion.398
  14.4 2.9 %collective-permute-start.2 = (f32[5,6,3,1024]{3,1,2,0:T(8,128)}, f32[5,6,3,1024]{3,1,2,0:T(8,128)}, u32[]{:S(2)}, u32[]{:S(2)}) collective-permute-start(f32[5,6,3,1024]{3,1,2,0:T(8,128)} %get-tuple-element.204), channel_id=1, source_target_pairs={{1,0},{2,1},{3,2},{5,4},{6,5},{7,6},{9,8},{10,9},{11,10},{13,12},{... | collective-permute-start | bytes 1105928 | tf_op jit(solution)/shard_map/ppermute | solution.py:21
  17.2 3.0 %collective-permute-start.1 = (f32[5,6,3,1024]{3,1,2,0:T(8,128)}, f32[5,6,3,1024]{3,1,2,0:T(8,128)}, u32[]{:S(2)}, u32[]{:S(2)}) collective-permute-start(f32[5,6,3,1024]{3,1,2,0:T(8,128)} %get-tuple-element.203), channel_id=1, source_target_pairs={{0,1},{1,2},{2,3},{4,5},{5,6},{6,7},{8,9},{9,10},{10,11},{12,13},{... | collective-permute-start | bytes 1105928 | tf_op jit(solution)/shard_map/ppermute | solution.py:19
  20.5 1.1 copy.43
  21.6 1.2 collective-permute-start
  22.8 0.7 fusion.397
  23.4 0.8 fusion.396
  24.9 1.7 %slice_bitcast_fusion.1 = (f32[5,8,1024]{2,1,0:T(8,128)}, f32[5,8,1024]{2,1,0:T(8,128)}) fusion(f32[5,6,8,1024]{3,2,1,0:T(8,128)} %param.16), kind=kLoop, calls=%fused_computation.697 | loop fusion | bytes 655360 | tf_op jit(solution)/shard_map/slice | solution.py:213
  26.6 0.7 reverse_negate_fusion
  27.3 0.6 slice.1344
  28.0 1.5 slice.1336
  29.5 1.0 slice.1332
  30.6 2.5 %concatenate.83 = f32[5,6,8,1030]{3,1,2,0:T(8,128)} concatenate(f32[5,6,8,3]{3,1,2,0:T(8,128)S(1)} %collective-permute-done.3, f32[5,6,8,1024]{3,1,2,0:T(8,128)S(1)} %get-tuple-element.209, f32[5,6,8,3]{3,1,2,0:T(8,128)} %collective-permute-done.4), dimensions={3} | concatenate | bytes 1977600 | tf_op jit(solution)/shard_map/concatenate | solution.py:17
  33.1 1.1 fusion.350
  34.2 1.6 %broadcast_multiply_fusion.2 = f32[5,6,8,1030]{3,1,2,0:T(8,128)S(1)} fusion(f32[5,6,8,1030]{3,1,2,0:T(8,128)} %concatenate.83, f32[6,8,1030]{2,0,1:T(8,128)S(1)} %fusion.350), kind=kLoop, calls=%fused_computation.177 | loop fusion | flops 247200 | bytes 2175360 | tf_op jit(solution)/shard_map/mul | solution.py:46
  36.3 0.9 constant_dynamic-update-slice_fusion.2
  37.2 0.5 fusion.6
  37.7 9.0 %constant_dynamic-update-slice_fusion.3 = (f32[5,6,8,1025]{3,1,2,0:T(8,128)S(1)}, f32[1,6,8,1025]{3,1,2,0:T(8,128)S(1)}, f32[1,6,8,1025]{3,1,2,0:T(8,128)S(1)}, ...) fusion(f32[5,6,8,1027]{3,1,2,0:T(8,128)S(1)} %constant_dynamic-, ...), kind=kLoop, calls=%fused_computation.704 | loop fusion | flops 36654000 | bytes 18493632
  46.7 2.2 %add_dynamic-update-slice_fusion.3 = (f32[5,6,8,1025]{3,1,2,0:T(8,128)S(1)}, f32[1,6,8,1025]{3,1,2,0:T(8,128)S(1)}) fusion(f32[5,6,8,1025]{3,1,2,0:T(8,128)S(1)} %get-tuple-element.169, f32[1,6,8,1025]{3,1,2,0:T(8,128)S(1)} %get-tuple-element.186, f32[1,6,8,1025]{3,1,2,0:T(8,128)S(1)} %get-tuple-element.170, f32[1,6,8,1025]{3,1,2,0:T(8,128)S(1)} %get-tuple-element.192, ...), kind=kLoop, calls=%fused_computation.314 | loop fusion | flops 8659200 | bytes 9142272
  48.9 8.2 %add_dynamic-update-slice_fusion.2 = (f32[5,6,8,1025]{3,1,2,0:T(8,128)S(1)}, f32[1,6,8,1025]{3,1,2,0:T(8,128)S(1)}, f32[1,6,8,1025]{3,1,2,0:T(8,128)S(1)}, f32[1,6,8,1025]{3,1,2,0:T(8,128)S(1)}) fusion(f32[5,6,8,1025]{3,1,2,0:T(8,128)S(1)} %get-tuple-element.167, f32[1,6,8,1025]{3,1,2,0:T(8,128)S(1)} %get-tuple-element.173, ...), kind=kLoop, calls=%fused_computation.291 | loop fusion | flops 31734000 | bytes 13271040
  57.0 2.2 %add_dynamic-update-slice_fusion.1 = (f32[5,6,8,1025]{3,1,2,0:T(8,128)S(1)}, f32[1,6,8,1025]{3,1,2,0:T(8,128)S(1)}) fusion(f32[5,6,8,1025]{3,1,2,0:T(8,128)S(1)} %get-tuple-element.163, f32[1,6,8,1025]{3,1,2,0:T(8,128)S(1)} %get-tuple-element.187, f32[1,6,8,1025]{3,1,2,0:T(8,128)S(1)} %get-tuple-element.170, f32[1,6,8,1025]{3,1,2,0:T(8,128)S(1)} %get-tuple-element.192, ...), kind=kLoop, calls=%fused_computation.283 | loop fusion | flops 8659200 | bytes 9142272
  59.6 0.5 copy-done.45
  60.2 1.1 maximum_select_fusion.1
  61.3 1.1 maximum_select_fusion
  64.1 11.1 %constant_dynamic-update-slice_fusion.1 = (f32[5,6,9,1024]{3,1,2,0:T(8,128)S(1)}, f32[1,6,9,1024]{3,1,2,0:T(8,128)S(1)}, f32[1,6,9,1024]{3,1,2,0:T(8,128)}, f32[...) fusion(f32[1,6,14,1024]{3,1,2,0:T(8,128)S(1)} %get-tuple-elemen, ...), kind=kLoop, calls=%fused_computation.702 | loop fusion | flops 42190848 | bytes 17276928
  75.3 2.8 %add_dynamic-update-slice_fusion.7 = (f32[5,6,9,1024]{3,1,2,0:T(8,128)S(1)}, f32[1,6,9,1024]{3,1,2,0:T(8,128)}) fusion(f32[5,6,9,1024]{3,1,2,0:T(8,128)S(1)} %get-tuple-element.127, f32[1,6,9,1024]{3,1,2,0:T(8,128)S(1)} %get-tuple-element.144, f32[1,6,9,1024]{3,1,2,0:T(8,128)S(1)} %get-tuple-element.128, f32[1,6,9,1024]{3,1,2,0:T(8,128)S(1)} %get-tuple-element.154, ...), kind=kLoop, calls=%fused_computation.434 | loop fusion | flops 9897984 | bytes 9003008
  78.1 1.2 copy-done.4
  79.6 4.8 %add_dynamic-update-slice_fusion.6 = (f32[5,6,9,1024]{3,1,2,0:T(8,128)}, f32[1,6,9,1024]{3,1,2,0:T(8,128)S(1)}) fusion(f32[5,6,9,1024]{3,1,2,0:T(8,128)} %copy-done.4, f32[1,6,9,1024]{3,1,2,0:T(8,128)} %get-tuple-element.145, f32[1,6,9,1024]{3,1,2,0:T(8,128)} %copy-done.22, f32[1,6,9,1024]{3,1,2,0:T(8,128)} %copy-done.13, f32[1,6,9,1024]{3,1,2,0:T(8,128)} %copy-done.11, ...), kind=kLoop, calls=%fused_computation.426 | loop fusion | flops 9897984 | bytes 8282112
  84.8 8.5 %add_dynamic-update-slice_fusion.5 = (f32[5,6,9,1024]{3,1,2,0:T(8,128)}, f32[1,6,9,1024]{3,1,2,0:T(8,128)S(1)}, f32[1,6,9,1024]{3,1,2,0:T(8,128)S(1)}, f32[1,6,9,1024]{3,1,2,0:T(8,128)S(1)}) fusion(f32[5,6,9,1024]{3,1,2,0:T(8,128)} %get-tuple-element.123, f32[1,6,9,1024]{3,1,2,0:T(8,128)S(1)} %copy-done.24, f32[1,6,9,1024]{3,1,2,0:T(8,128)S(1)} %copy-done.23, ...), kind=kLoop, calls=%fused_computation.403 | loop fusion | flops 35665920 | bytes 10321920
  93.3 2.2 %add_dynamic-update-slice_fusion.4 = f32[5,6,9,1024]{3,1,2,0:T(8,128)} fusion(f32[5,6,9,1024]{3,1,2,0:T(8,128)} %get-tuple-element.119, f32[1,6,9,1024]{3,1,2,0:T(8,128)S(1)} %get-tuple-element.122, f32[1,6,9,1024]{3,1,2,0:T(8,128)S(1)} %copy-done.21, f32[1,6,9,1024]{3,1,2,0:T(8,128)S(1)} %get-tuple-element.124, f32[1,6,9,1024]{3,1,2,0:T(8,128)S(1)} %copy-done.20, ...), kind=kLoop, calls=%fused_computation.402 | loop fusion | flops 1161216 | bytes 3096576 | tf_op jit(solution)/shard_map/stack | solution.py:161
  95.5 27.8 %all-gather.2.cloned.1.call-done = f32[5,3,8,4096]{3,2,1,0:T(8,128)} async-done(((f32[5,3,8,1024]{3,2,1,0:T(8,128)}), f32[5,3,8,4096]{3,2,1,0:T(8,128)}) %all-gather.2.cloned.1.call-update) | async-done | bytes 1966096 | tf_op jit(solution)/shard_map/all_gather | solution.py:203
  123.3 1.3 fusion.17
  124.6 1.5 rev.2
  126.6 0.5 copy-done.42
  127.1 0.5 copy_select_fusion.1
  127.7 0.6 pad_maximum_fusion
  128.2 0.6 fusion.9
  128.9 0.6 broadcast_multiply_fusion
  130.0 8.7 %constant_dynamic-update-slice_fusion = (f32[5,7,8,1024]{3,1,2,0:T(8,128)S(1)}, f32[1,7,8,1024]{3,1,2,0:T(8,128)S(1)}, f32[1,7,8,1024]{3,1,2,0:T(8,128)S(1)}, f3...) fusion(f32[1,12,8,1024]{3,1,2,0:T(8,128)S(1)} %get-tuple-elemen, ...), kind=kLoop, calls=%fused_computation.701 | loop fusion | flops 43753472 | bytes 18382848
  138.7 6.8 %add_dynamic-update-slice_fusion.11 = (f32[5,7,8,1024]{3,1,2,0:T(8,128)S(1)}, f32[1,7,8,1024]{3,1,2,0:T(8,128)S(1)}, f32[1,7,8,1024]{3,1,2,0:T(8,128)S(1)}, f32[1,7,8,1024]{3,1,2,0:T(8,128)S(1)}) fusion(f32[5,7,8,1024]{3,1,2,0:T(8,128)S(1)} %get-tuple-element.85, f32[1,7,8,1024]{3,1,2,0:T(8,128)S(1)} %get-tuple-element.89, ...), kind=kLoop, calls=%fused_computation.586 | loop fusion | flops 36986880 | bytes 11796480
  145.5 2.0 %add_dynamic-update-slice_fusion.10 = (f32[5,7,8,1024]{3,1,2,0:T(8,128)S(1)}, f32[1,7,8,1024]{3,1,2,0:T(8,128)S(1)}) fusion(f32[5,7,8,1024]{3,1,2,0:T(8,128)S(1)} %get-tuple-element.81, f32[1,7,8,1024]{3,1,2,0:T(8,128)S(1)} %get-tuple-element.102, f32[1,7,8,1024]{3,1,2,0:T(8,128)S(1)} %get-tuple-element.86, f32[1,7,8,1024]{3,1,2,0:T(8,128)S(1)} %get-tuple-element.112, ...), kind=kLoop, calls=%fused_computation.578 | loop fusion | flops 10264576 | bytes 8650752
  147.5 2.0 %add_dynamic-update-slice_fusion.9 = (f32[5,7,8,1024]{3,1,2,0:T(8,128)S(1)}, f32[1,7,8,1024]{3,1,2,0:T(8,128)S(1)}) fusion(f32[5,7,8,1024]{3,1,2,0:T(8,128)S(1)} %get-tuple-element.79, f32[1,7,8,1024]{3,1,2,0:T(8,128)S(1)} %get-tuple-element.103, f32[1,7,8,1024]{3,1,2,0:T(8,128)S(1)} %get-tuple-element.86, f32[1,7,8,1024]{3,1,2,0:T(8,128)S(1)} %get-tuple-element.112, ...), kind=kLoop, calls=%fused_computation.570 | loop fusion | flops 10264576 | bytes 8650752
  150.0 1.0 copy-done.5
  151.4 2.0 %fusion.15 = f32[5,6,8,1024]{3,1,2,0:T(8,128)S(1)} fusion(f32[5,6,8,1025]{3,1,2,0:T(8,128)S(1)} %copy-done.7, f32[5,6,9,1024]{3,1,2,0:T(8,128)S(1)} %copy-done.5, f32[5,7,8,1024]{3,1,2,0:T(8,128)S(1)} %add_dynamic-update-slice_fusion.8, f32[5,6,8,1024]{3,2,1,0:T(8,128)S(1)} %copy-done.41, f32[5,6,8,1024]{3,2,1,0:T(8,128)S(1)} %copy-done.8), kind=kLoop, calls=%fused_computation.169 | loop fusion | flops 2457600 | bytes 8847360 | tf_op jit(solution)/shard_map/add | solution.py:225
  153.4 1.5 copy.66
  (119 shorter events, 4.9 us)
Async XLA Ops:
  6.5 116.8 %all-gather.2.cloned.1.call-start = ((), (), s32[]{:S(2)}) async-start(), calls=%async_computation | async-start | bytes 2457600 | tf_op jit(solution)/shard_map/all_gather | solution.py:203
  9.2 21.4 %collective-permute-start.4 = (f32[5,6,8,3]{3,1,2,0:T(8,128)}, f32[5,6,8,3]{3,1,2,0:T(8,128)}, u32[]{:S(2)}, u32[]{:S(2)}) collective-permute-start(f32[5,6,8,3]{3,1,2,0:T(8,128)} %get-tuple-element.206), channel_id=1, source_target_pairs={{4,0},{8,4},{12,8},{0,12},{5,1},{9,5},{13,9},{1,13},{6,2},{10,6},{... | collective-permute-start | bytes 8648 | tf_op jit(solution)/shard_map/ppermute | solution.py:21
  13.3 17.2 %collective-permute-start.3 = (f32[5,6,8,3]{3,1,2,0:T(8,128)}, f32[5,6,8,3]{3,1,2,0:T(8,128)S(1)}, u32[]{:S(2)}, u32[]{:S(2)}) collective-permute-start(f32[5,6,8,3]{3,1,2,0:T(8,128)} %get-tuple-element.205), channel_id=1, source_target_pairs={{0,4},{4,8},{8,12},{12,0},{1,5},{5,9},{9,13},{13,1},{2,6},{6,10},{... | collective-permute-start | bytes 8648 | tf_op jit(solution)/shard_map/ppermute | solution.py:19
  14.4 45.2 %collective-permute-start.2 = (f32[5,6,3,1024]{3,1,2,0:T(8,128)}, f32[5,6,3,1024]{3,1,2,0:T(8,128)}, u32[]{:S(2)}, u32[]{:S(2)}) collective-permute-start(f32[5,6,3,1024]{3,1,2,0:T(8,128)} %get-tuple-element.204), channel_id=1, source_target_pairs={{1,0},{2,1},{3,2},{5,4},{6,5},{7,6},{9,8},{10,9},{11,10},{13,12},{... | collective-permute-start | bytes 1105928 | tf_op jit(solution)/shard_map/ppermute | solution.py:21
  17.2 44.1 %collective-permute-start.1 = (f32[5,6,3,1024]{3,1,2,0:T(8,128)}, f32[5,6,3,1024]{3,1,2,0:T(8,128)}, u32[]{:S(2)}, u32[]{:S(2)}) collective-permute-start(f32[5,6,3,1024]{3,1,2,0:T(8,128)} %get-tuple-element.203), channel_id=1, source_target_pairs={{0,1},{1,2},{2,3},{4,5},{5,6},{6,7},{8,9},{9,10},{10,11},{12,13},{... | collective-permute-start | bytes 1105928 | tf_op jit(solution)/shard_map/ppermute | solution.py:19
  21.6 57.8 %collective-permute-start = (f32[5,3,8,1024]{3,2,1,0:T(8,128)}, f32[5,3,8,1024]{3,2,1,0:T(8,128)}, u32[]{:S(2)}, u32[]{:S(2)}) collective-permute-start(f32[5,3,8,1024]{3,2,1,0:T(8,128)} %copy.43), channel_id=1, source_target_pairs={{0,16},{16,0},{1,17},{17,1},{2,18},{18,2},{3,19},{19,3},{4,20},{20... | collective-permute-start | bytes 1474568 | tf_op jit(solution)/shard_map/ppermute | solution.py:35
  34.2 1.8 %copy-start.2 = (f32[5,6,8,1030]{3,1,2,0:T(8,128)S(1)}, f32[5,6,8,1030]{3,1,2,0:T(8,128)}, u32[]{:S(2)}) copy-start(f32[5,6,8,1030]{3,1,2,0:T(8,128)} %concatenate.83) | copy-start | bytes 2966404
  59.6 1.7 %copy-start.6 = (f32[5,6,8,1025]{3,1,2,0:T(8,128)}, f32[5,6,8,1025]{3,1,2,0:T(8,128)S(1)}, u32[]{:S(2)}) copy-start(f32[5,6,8,1025]{3,1,2,0:T(8,128)S(1)} %add_dynamic-update-slice_fusion) | copy-start | bytes 2952004
  59.6 1.7 %copy-start.44 = (f32[1,6,3,1024]{3,1,2,0:T(8,128)S(1)}, f32[1,6,3,1024]{3,1,2,0:T(8,128)}, u32[]{:S(2)}) copy-start(f32[1,6,3,1024]{3,1,2,0:T(8,128)} %slice.1336) | copy-start | bytes 221188
  59.6 1.7 %copy-start.46 = (f32[1,6,3,1024]{3,1,2,0:T(8,128)S(1)}, f32[1,6,3,1024]{3,1,2,0:T(8,128)}, u32[]{:S(2)}) copy-start(f32[1,6,3,1024]{3,1,2,0:T(8,128)} %get-tuple-element.216) | copy-start | bytes 221188
  63.5 11.8 %copy-start = (f32[5,6,14,1024]{3,1,2,0:T(8,128)}, f32[5,6,14,1024]{3,1,2,0:T(8,128)S(1)}, u32[]{:S(2)}) copy-start(f32[5,6,14,1024]{3,1,2,0:T(8,128)S(1)} %broadcast_multiply_fusion.1) | copy-start | bytes 5160964
  75.2 2.9 %copy-start.9 = (f32[1,6,9,1024]{3,1,2,0:T(8,128)}, f32[1,6,9,1024]{3,1,2,0:T(8,128)S(1)}, u32[]{:S(2)}) copy-start(f32[1,6,9,1024]{3,1,2,0:T(8,128)S(1)} %get-tuple-element.150) | copy-start | bytes 663556
  75.2 2.9 %copy-start.11 = (f32[1,6,9,1024]{3,1,2,0:T(8,128)}, f32[1,6,9,1024]{3,1,2,0:T(8,128)S(1)}, u32[]{:S(2)}) copy-start(f32[1,6,9,1024]{3,1,2,0:T(8,128)S(1)} %get-tuple-element.152) | copy-start | bytes 663556
  75.2 2.9 %copy-start.13 = (f32[1,6,9,1024]{3,1,2,0:T(8,128)}, f32[1,6,9,1024]{3,1,2,0:T(8,128)S(1)}, u32[]{:S(2)}) copy-start(f32[1,6,9,1024]{3,1,2,0:T(8,128)S(1)} %get-tuple-element.154) | copy-start | bytes 663556
  75.2 2.9 %copy-start.15 = (f32[1,6,9,1024]{3,1,2,0:T(8,128)}, f32[1,6,9,1024]{3,1,2,0:T(8,128)S(1)}, u32[]{:S(2)}) copy-start(f32[1,6,9,1024]{3,1,2,0:T(8,128)S(1)} %get-tuple-element.156) | copy-start | bytes 663556
  75.3 2.9 %copy-start.17 = (f32[1,6,9,1024]{3,1,2,0:T(8,128)}, f32[1,6,9,1024]{3,1,2,0:T(8,128)S(1)}, u32[]{:S(2)}) copy-start(f32[1,6,9,1024]{3,1,2,0:T(8,128)S(1)} %get-tuple-element.158) | copy-start | bytes 663556
  75.3 2.9 %copy-start.19 = (f32[1,6,9,1024]{3,1,2,0:T(8,128)}, f32[1,6,9,1024]{3,1,2,0:T(8,128)S(1)}, u32[]{:S(2)}) copy-start(f32[1,6,9,1024]{3,1,2,0:T(8,128)S(1)} %get-tuple-element.144) | copy-start | bytes 663556
  75.3 2.9 %copy-start.22 = (f32[1,6,9,1024]{3,1,2,0:T(8,128)}, f32[1,6,9,1024]{3,1,2,0:T(8,128)S(1)}, u32[]{:S(2)}) copy-start(f32[1,6,9,1024]{3,1,2,0:T(8,128)S(1)} %get-tuple-element.128) | copy-start | bytes 663556
  79.4 5.0 %copy-start.1 = (f32[5,6,14,1024]{3,1,2,0:T(8,128)S(1)}, f32[5,6,14,1024]{3,1,2,0:T(8,128)}, u32[]{:S(2)}) copy-start(f32[5,6,14,1024]{3,1,2,0:T(8,128)} %copy-done) | copy-start | bytes 5160964
  79.4 5.0 %copy-start.10 = (f32[1,6,9,1024]{3,1,2,0:T(8,128)S(1)}, f32[1,6,9,1024]{3,1,2,0:T(8,128)}, u32[]{:S(2)}) copy-start(f32[1,6,9,1024]{3,1,2,0:T(8,128)} %copy-done.9) | copy-start | bytes 663556
  79.4 5.0 %copy-start.12 = (f32[1,6,9,1024]{3,1,2,0:T(8,128)S(1)}, f32[1,6,9,1024]{3,1,2,0:T(8,128)}, u32[]{:S(2)}) copy-start(f32[1,6,9,1024]{3,1,2,0:T(8,128)} %copy-done.11) | copy-start | bytes 663556
  79.4 5.0 %copy-start.14 = (f32[1,6,9,1024]{3,1,2,0:T(8,128)S(1)}, f32[1,6,9,1024]{3,1,2,0:T(8,128)}, u32[]{:S(2)}) copy-start(f32[1,6,9,1024]{3,1,2,0:T(8,128)} %copy-done.13) | copy-start | bytes 663556
  79.4 5.0 %copy-start.16 = (f32[1,6,9,1024]{3,1,2,0:T(8,128)S(1)}, f32[1,6,9,1024]{3,1,2,0:T(8,128)}, u32[]{:S(2)}) copy-start(f32[1,6,9,1024]{3,1,2,0:T(8,128)} %copy-done.15) | copy-start | bytes 663556
  79.4 5.0 %copy-start.18 = (f32[1,6,9,1024]{3,1,2,0:T(8,128)S(1)}, f32[1,6,9,1024]{3,1,2,0:T(8,128)}, u32[]{:S(2)}) copy-start(f32[1,6,9,1024]{3,1,2,0:T(8,128)} %copy-done.17) | copy-start | bytes 663556
  79.4 5.0 %copy-start.20 = (f32[1,6,9,1024]{3,1,2,0:T(8,128)S(1)}, f32[1,6,9,1024]{3,1,2,0:T(8,128)}, u32[]{:S(2)}) copy-start(f32[1,6,9,1024]{3,1,2,0:T(8,128)} %copy-done.19) | copy-start | bytes 663556
  79.4 5.0 %copy-start.21 = (f32[1,6,9,1024]{3,1,2,0:T(8,128)S(1)}, f32[1,6,9,1024]{3,1,2,0:T(8,128)}, u32[]{:S(2)}) copy-start(f32[1,6,9,1024]{3,1,2,0:T(8,128)} %get-tuple-element.145) | copy-start | bytes 663556
  79.4 5.0 %copy-start.23 = (f32[1,6,9,1024]{3,1,2,0:T(8,128)S(1)}, f32[1,6,9,1024]{3,1,2,0:T(8,128)}, u32[]{:S(2)}) copy-start(f32[1,6,9,1024]{3,1,2,0:T(8,128)} %get-tuple-element.129) | copy-start | bytes 663556
  79.4 5.0 %copy-start.24 = (f32[1,6,9,1024]{3,1,2,0:T(8,128)S(1)}, f32[1,6,9,1024]{3,1,2,0:T(8,128)}, u32[]{:S(2)}) copy-start(f32[1,6,9,1024]{3,1,2,0:T(8,128)} %get-tuple-element.131) | copy-start | bytes 663556
  79.5 5.0 %copy-start.26 = (f32[1,6,9,1024]{3,1,2,0:T(8,128)S(1)}, f32[1,6,9,1024]{3,1,2,0:T(8,128)}, u32[]{:S(2)}) copy-start(f32[1,6,9,1024]{3,1,2,0:T(8,128)} %get-tuple-element.132) | copy-start | bytes 663556
  79.5 5.0 %copy-start.27 = (f32[1,6,9,1024]{3,1,2,0:T(8,128)S(1)}, f32[1,6,9,1024]{3,1,2,0:T(8,128)}, u32[]{:S(2)}) copy-start(f32[1,6,9,1024]{3,1,2,0:T(8,128)} %get-tuple-element.133) | copy-start | bytes 663556
  79.5 5.0 %copy-start.28 = (f32[1,6,9,1024]{3,1,2,0:T(8,128)S(1)}, f32[1,6,9,1024]{3,1,2,0:T(8,128)}, u32[]{:S(2)}) copy-start(f32[1,6,9,1024]{3,1,2,0:T(8,128)} %get-tuple-element.134) | copy-start | bytes 663556
  79.5 5.0 %copy-start.29 = (f32[1,6,9,1024]{3,1,2,0:T(8,128)S(1)}, f32[1,6,9,1024]{3,1,2,0:T(8,128)}, u32[]{:S(2)}) copy-start(f32[1,6,9,1024]{3,1,2,0:T(8,128)} %get-tuple-element.135) | copy-start | bytes 663556
  79.5 5.0 %copy-start.30 = (f32[1,6,9,1024]{3,1,2,0:T(8,128)S(1)}, f32[1,6,9,1024]{3,1,2,0:T(8,128)}, u32[]{:S(2)}) copy-start(f32[1,6,9,1024]{3,1,2,0:T(8,128)} %get-tuple-element.136) | copy-start | bytes 663556
  79.5 5.0 %copy-start.31 = (f32[1,6,9,1024]{3,1,2,0:T(8,128)S(1)}, f32[1,6,9,1024]{3,1,2,0:T(8,128)}, u32[]{:S(2)}) copy-start(f32[1,6,9,1024]{3,1,2,0:T(8,128)} %get-tuple-element.137) | copy-start | bytes 663556
  79.5 5.0 %copy-start.32 = (f32[1,6,9,1024]{3,1,2,0:T(8,128)S(1)}, f32[1,6,9,1024]{3,1,2,0:T(8,128)}, u32[]{:S(2)}) copy-start(f32[1,6,9,1024]{3,1,2,0:T(8,128)} %get-tuple-element.138) | copy-start | bytes 663556
  79.5 5.0 %copy-start.33 = (f32[1,6,9,1024]{3,1,2,0:T(8,128)S(1)}, f32[1,6,9,1024]{3,1,2,0:T(8,128)}, u32[]{:S(2)}) copy-start(f32[1,6,9,1024]{3,1,2,0:T(8,128)} %get-tuple-element.139) | copy-start | bytes 663556
  79.5 5.0 %copy-start.34 = (f32[1,6,9,1024]{3,1,2,0:T(8,128)S(1)}, f32[1,6,9,1024]{3,1,2,0:T(8,128)}, u32[]{:S(2)}) copy-start(f32[1,6,9,1024]{3,1,2,0:T(8,128)} %get-tuple-element.140) | copy-start | bytes 663556
  79.5 5.0 %copy-start.35 = (f32[1,6,9,1024]{3,1,2,0:T(8,128)S(1)}, f32[1,6,9,1024]{3,1,2,0:T(8,128)}, u32[]{:S(2)}) copy-start(f32[1,6,9,1024]{3,1,2,0:T(8,128)} %get-tuple-element.141) | copy-start | bytes 663556
  79.6 5.0 %copy-start.36 = (f32[1,6,9,1024]{3,1,2,0:T(8,128)S(1)}, f32[1,6,9,1024]{3,1,2,0:T(8,128)}, u32[]{:S(2)}) copy-start(f32[1,6,9,1024]{3,1,2,0:T(8,128)} %get-tuple-element.142) | copy-start | bytes 663556
  79.6 5.0 %copy-start.37 = (f32[1,6,9,1024]{3,1,2,0:T(8,128)S(1)}, f32[1,6,9,1024]{3,1,2,0:T(8,128)}, u32[]{:S(2)}) copy-start(f32[1,6,9,1024]{3,1,2,0:T(8,128)} %get-tuple-element.143) | copy-start | bytes 663556
  79.6 5.2 %copy-start.38 = (f32[1,6,9,1024]{3,1,2,0:T(8,128)S(1)}, f32[1,6,9,1024]{3,1,2,0:T(8,128)}, u32[]{:S(2)}) copy-start(f32[1,6,9,1024]{3,1,2,0:T(8,128)} %get-tuple-element.147) | copy-start | bytes 663556
  79.6 5.2 %copy-start.39 = (f32[1,6,9,1024]{3,1,2,0:T(8,128)S(1)}, f32[1,6,9,1024]{3,1,2,0:T(8,128)}, u32[]{:S(2)}) copy-start(f32[1,6,9,1024]{3,1,2,0:T(8,128)} %get-tuple-element.149) | copy-start | bytes 663556
  84.8 8.5 %copy-start.25 = (f32[1,6,9,1024]{3,1,2,0:T(8,128)S(1)}, f32[1,6,9,1024]{3,1,2,0:T(8,128)}, u32[]{:S(2)}) copy-start(f32[1,6,9,1024]{3,1,2,0:T(8,128)} %get-tuple-element.126) | copy-start | bytes 663556
  84.8 8.5 %copy-start.40 = (f32[1,6,9,1024]{3,1,2,0:T(8,128)S(1)}, f32[1,6,9,1024]{3,1,2,0:T(8,128)}, u32[]{:S(2)}) copy-start(f32[1,6,9,1024]{3,1,2,0:T(8,128)} %get-tuple-element.130) | copy-start | bytes 663556
  147.5 2.4 %copy-start.8 = (f32[5,6,8,1024]{3,2,1,0:T(8,128)S(1)}, f32[5,6,8,1024]{3,2,1,0:T(8,128)}, u32[]{:S(2)}) copy-start(f32[5,6,8,1024]{3,2,1,0:T(8,128)} %param.16) | copy-start | bytes 2949124
  147.5 2.4 %copy-start.41 = (f32[5,6,8,1024]{3,2,1,0:T(8,128)S(1)}, f32[5,6,8,1024]{3,2,1,0:T(8,128)}, u32[]{:S(2)}) copy-start(f32[5,6,8,1024]{3,2,1,0:T(8,128)} %param.15) | copy-start | bytes 2949124
  149.6 1.4 copy-start.5
  149.6 1.8 %copy-start.7 = (f32[5,6,8,1025]{3,1,2,0:T(8,128)S(1)}, f32[5,6,8,1025]{3,1,2,0:T(8,128)}, u32[]{:S(2)}) copy-start(f32[5,6,8,1025]{3,1,2,0:T(8,128)} %copy-done.6) | copy-start | bytes 2952004
  (6 other events, 6.1 us)
Sparse Core Ops, SparseCore 0:
  79.5 43.7 all-gather.1
where the time goes:
time: 163 us; the launch traced here: 162 us
  other arithmetic  85.6 us (53%)
  waiting for transfers between devices  27.8 us (17%)
  local copies, waits for them, and re-layouts  22.1 us (14%)
  between operations  15 us (9%)
  starting transfers between devices  11.3 us (7%)
    unnamed x12, other arithmetic  68.1 us
    all_gather x1, waiting for transfers between devices, shards(): whole = lax.all_gather(facing, 'theta', axis=3, tiled=True)  27.8 us
    ppermute x2, starting transfers between devices, padded_2(): lax.ppermute(head, axis, [((i + 1) % count, i) for i in range(ends)])  7 us
    unnamed x97, local copies, waits for them, and re-layouts  6.38 us
    slice x6, local copies, waits for them, and re-layouts, flip_radial(): return jnp.concatenate([turned[:3], -turned[3:4], turned[4:]], axis=0)  4.59 us
    mul x6, other arithmetic, euler_flux(): flux = state * velocity[None]  3.87 us
    concatenate x2, local copies, waits for them, and re-layouts, padded_2(): jnp.concatenate([lax.ppermute(tail, axis, [(i, (i + 1) % count) for i in...  3.47 us
  transfers between devices with their start and end apart: 6, of which 1 were waited for; matrix products, arithmetic and copies ran while one was open for 44% of the time, Pallas kernels for 0%

commit v1 on v0

v1 whole, which is shorter than its diff:
```python
import functools

import jax
import jax.numpy as jnp
from jax import lax
from jax.experimental import pallas as pl
from jax.experimental.pallas import tpu as pltpu
from jax.sharding import PartitionSpec as P

gamma_ratio = 1.4
weno_epsilon = 1e-06
step_ratio = 0.12
lanes = 128
ghosts = 3
group = 16
flux_scale = 12.0
vmem_bytes = 48 * 1024 * 1024

axial_order = (0, 1, 2, 3, 4)
radial_order = (0, 3, 1, 2, 4)
theta_order = (0, 2, 1, 3, 4)


def inverse(value):
    guess = pl.reciprocal(value, approx=True)
    return guess * (2.0 - value * guess)


def cell_terms(state):
    density, normal, first, second, energy = state
    inv = inverse(density)
    speed = normal * inv
    kinetic = 0.5 * (normal * normal + first * first + second * second) * inv
    pressure = (gamma_ratio - 1.0) * (energy - kinetic)
    square = gamma_ratio * pressure * inv
    wave = jnp.abs(speed) + square * lax.rsqrt(square)
    flux = (normal, normal * speed + pressure, first * speed, second * speed, (energy + pressure) * speed)
    return flux, wave


def interface_terms(left, right):
    (state_l, flux_l, wave_l), (state_r, flux_r, wave_r) = left, right
    return (
        [r - l for l, r in zip(state_l, state_r)]
        + [r - l for l, r in zip(flux_l, flux_r)]
        + [r + l for l, r in zip(state_l, state_r)]
        + [r + l for l, r in zip(flux_l, flux_r)]
        + [jnp.maximum(wave_l, wave_r)]
    )


def weno_terms(d0, d1, d2, d3, epsilon):
    e0 = d1 - d0
    e1 = d2 - d1
    e2 = d3 - d2
    t1 = 0.75 * d1
    t2 = 0.75 * d2
    q1 = t1 * d1 + epsilon
    q2 = t2 * d2 + epsilon
    low = (e0 + t1) * e0 + q1
    mid = (e1 + t1) * e1 + q1
    high = (e2 - t2) * e2 + q2
    x = mid * pl.reciprocal(low, approx=True)
    y = mid * pl.reciprocal(high, approx=True)
    weight_low = x * x
    weight_high = 1.5 * (y * y)
    total = 0.5 * weight_low + (weight_high + 3.0)
    return (weight_low * (e0 - e1) + weight_high * (e1 - e2)) * pl.reciprocal(total, approx=True)


def face_terms(diff_state, diff_flux, sum_state, sum_flux, wave):
    inv = inverse(sum_state[0])
    un, va, vb, specific = (inv * part for part in sum_state[1:])
    half = 0.5 * (un * un + va * va + vb * vb)
    internal = specific - half
    square = gamma_ratio * (gamma_ratio - 1.0) * internal
    inv_sound = lax.rsqrt(square)
    sound = square * inv_sound
    factor = (gamma_ratio - 1.0) * inv_sound * inv_sound
    enthalpy = specific + (gamma_ratio - 1.0) * internal

    def project(dens, norm, first, second, energy):
        sn = norm - un * dens
        sa = first - va * dens
        sb = second - vb * dens
        even = factor * (energy - half * dens - un * sn - va * sa - vb * sb)
        odd = inv_sound * sn
        return even - odd, dens - even, sa, sb, even + odd

    damped = [[wave * part for part in parts] for parts in diff_state]
    plus = [project(*(f + d for f, d in zip(diff_flux[s], damped[s]))) for s in range(4)]
    minus = [project(*(f - d for f, d in zip(diff_flux[s], damped[s]))) for s in range(1, 5)]
    fields = []
    for k in range(5):
        epsilon = weno_epsilon * (12.0 if k in (0, 4) else 3.0)
        p0, p1, p2, p3 = (plus[s][k] for s in range(4))
        m1, m2, m3, m4 = (minus[s][k] for s in range(4))
        linear = (p1 - m3) + 2.0 * (p2 - m2)
        fields.append(linear + weno_terms(p0, p1, p2, p3, epsilon) - weno_terms(m4, m3, m2, m1, epsilon))
    wave_minus, entropy, sa, sb, wave_plus = fields
    even = 0.5 * (wave_plus + wave_minus)
    odd = sound * (0.5 * (wave_plus - wave_minus))
    carried = even + entropy
    central = [0.5 * flux_scale * (f - d) for f, d in zip(sum_flux, damped[2])]
    return (
        central[0] + carried,
        central[1] + un * carried + odd,
        central[2] + va * carried + sa,
        central[3] + vb * carried + sb,
        central[4] + enthalpy * even + un * odd + half * entropy + va * sa + vb * sb,
    )


def with_terms(state):
    return (state, *cell_terms(state))


def lane_index(shape):
    return lax.broadcasted_iota(jnp.int32, shape, len(shape) - 1)


def pack_kernel(section, theta_low, theta_high, radial_low, radial_high, rows):
    planes, bands, width = section.shape[1:]
    tiles = width // lanes
    lane = lane_index((bands, lanes))
    for c in range(5):
        first = jnp.zeros((bands, lanes), jnp.float32)
        last = jnp.zeros((bands, lanes), jnp.float32)
        for p in range(planes):
            here = (lane >= group * p) & (lane < group * p + ghosts)
            head = section[c, p, :, 0:lanes]
            tail = section[c, p, :, width - lanes : width]
            first = jnp.where(here, pltpu.roll(head, group * p, 1) if p else head, first)
            last = jnp.where(here, pltpu.roll(tail, group * p + ghosts, 1), last)
        theta_low[c] = first
        theta_high[c] = last
    for c in range(5):

        def plane(p, carry):
            for j in range(tiles):
                rows[j * bands : (j + 1) * bands] = section[c, p, :, j * lanes : (j + 1) * lanes]
            for k in range(ghosts):
                radial_low[c, p, k] = rows[pl.ds(k, tiles, stride=bands)]
                radial_high[c, p, k] = rows[pl.ds(bands - ghosts + k, tiles, stride=bands)]
            return carry

        lax.fori_loop(0, planes, plane, 0)


def pack(section):
    _, planes, bands, width = section.shape
    tiles = width // lanes
    theta = jax.ShapeDtypeStruct((5, bands, lanes), jnp.float32)
    radial = jax.ShapeDtypeStruct((5, planes, ghosts, tiles, lanes), jnp.float32)
    return pl.pallas_call(
        pack_kernel,
        out_shape=(theta, theta, radial, radial),
        scratch_shapes=[pltpu.VMEM((bands * tiles, lanes), jnp.float32)],
        compiler_params=pltpu.CompilerParams(vmem_limit_bytes=vmem_bytes),
        name="pack",
    )(section)


batch = 2


def main_kernel(
    ids, section, own_low, left_high, right_low, low_radial, high_radial, acc, rows, turned, terms, side, strip
):
    planes, bands, width = section.shape[1:]
    tiles = width // lanes
    radial_pass(ids, section, low_radial, high_radial, rows, turned, terms)
    theta_pass(section, own_low, left_high, right_low, acc, rows, terms, side, strip)
    axial_inner(ids, section, acc, terms)


def radial_pass(ids, section, low_radial, high_radial, rows, turned, terms):
    planes, bands, width = section.shape[1:]
    tiles = width // lanes
    at_inner = ids[1] == 0
    at_outer = ids[1] == ids[2] - 1

    def spread(p, carry):
        for c in range(5):
            for j in range(tiles):
                rows[c, p, j * bands : (j + 1) * bands] = section[c, p, :, j * lanes : (j + 1) * lanes]
            for r in range(bands):
                turned[c, r + ghosts, p] = rows[c, p, pl.ds(r, tiles, stride=bands)]
            sign = -1.0 if c == 3 else 1.0
            for k in range(ghosts):
                wall_low = sign * rows[c, p, pl.ds(ghosts - 1 - k, tiles, stride=bands)]
                wall_high = sign * rows[c, p, pl.ds(bands - 1 - k, tiles, stride=bands)]
                turned[c, k, p] = jnp.where(at_inner, wall_low, low_radial[c, p, k])
                turned[c, bands + ghosts + k, p] = jnp.where(at_outer, wall_high, high_radial[c, p, k])
        return carry

    lax.fori_loop(0, planes, spread, 0)

    def pair(g, carry):
        p = g * batch

        def cell(r):
            return with_terms([turned[c, r, pl.ds(p, batch)] for c in radial_order])

        def interface(r, left):
            right = cell(r + 1)
            for n, value in enumerate(interface_terms(left, right)):
                terms[n, r] = value
            return right

        lax.fori_loop(0, bands + 2 * ghosts - 1, interface, cell(0))

        def face(r, before):
            flux = face_at(terms, r)
            for c, now, old in zip(radial_order, flux, before):

                @pl.when(r > 0)
                def _():
                    change = now - old
                    for b in range(batch):
                        rows[c, p + b, pl.ds(r - 1, tiles, stride=bands)] = change[b]

            return flux

        zero = tuple(jnp.zeros((batch, tiles, lanes), jnp.float32) for _ in range(5))
        lax.fori_loop(0, bands + 1, face, zero)
        return carry

    lax.fori_loop(0, planes // batch, pair, 0)


def face_at(terms, first):
    load = lambda n, r: terms[n, first + r]
    return face_terms(
        [[load(c, s) for c in range(5)] for s in range(5)],
        [[load(5 + c, s) for c in range(5)] for s in range(5)],
        [load(10 + c, 2) for c in range(5)],
        [load(15 + c, 2) for c in range(5)],
        load(20, 2),
    )


def shifted(before, here, after, shift, lane):
    if shift == 0:
        return here
    axis = here.ndim - 1
    if shift > 0:
        return pltpu.roll(jnp.where(lane < shift, after, here), lanes - shift, axis)
    return pltpu.roll(jnp.where(lane >= lanes + shift, before, here), -shift, axis)


def theta_pass(section, own_low, left_high, right_low, acc, rows, terms, side, strip):
    planes, bands, width = section.shape[1:]
    tiles = width // lanes
    lane = lane_index((bands, lanes))
    within = lane % group
    ends = with_terms(
        [jnp.where(within < ghosts, left_high[c], pltpu.roll(own_low[c], ghosts, 1)) for c in theta_order]
    )
    turn = lambda value: pltpu.roll(value, lanes - 1, 1)
    after = ([turn(v) for v in ends[0]], [turn(v) for v in ends[1]], turn(ends[2]))
    edge = interface_terms(ends, after)
    at = lambda n, s: edge[n] if s == 2 else pltpu.roll(edge[n], (2 - s) % lanes, 1)
    corner = face_terms(
        [[at(c, s) for c in range(5)] for s in range(5)],
        [[at(5 + c, s) for c in range(5)] for s in range(5)],
        [at(10 + c, 2) for c in range(5)],
        [at(15 + c, 2) for c in range(5)],
        at(20, 2),
    )
    for n, c in enumerate(theta_order):
        for p in range(planes):
            side[n, p] = pltpu.roll(corner[n], (lanes - 1 - (group * p + 2)) % lanes, 1)
            strip[n, 0, p] = pltpu.roll(left_high[c], (lanes - ghosts - group * p) % lanes, 1)
            strip[n, 1, p] = pltpu.roll(right_low[c], (-group * p) % lanes, 1)
    lane = lane_index((batch, bands, lanes))

    def pair(g, carry):
        p = g * batch

        def tile(t):
            start = pl.multiple_of(t * lanes, lanes)
            return [section[c, pl.ds(p, batch), :, pl.ds(start, lanes)] for c in theta_order]

        def store(t, left, right):
            shift = lambda a, b: shifted(None, a, b, 1, lane)
            moved = (
                [shift(a, b) for a, b in zip(left[0], right[0])],
                [shift(a, b) for a, b in zip(left[1], right[1])],
                shift(left[2], right[2]),
            )
            for n, value in enumerate(interface_terms(left, moved)):
                terms[n, t] = value

        def interface(t, left):
            right = with_terms(tile(t))
            store(t, left, right)
            return right

        low = with_terms([strip[n, 0, pl.ds(p, batch)] for n in range(5)])
        high = with_terms([strip[n, 1, pl.ds(p, batch)] for n in range(5)])
        last = lax.fori_loop(0, tiles, interface, low)
        store(tiles, last, high)
        store(tiles + 1, high, high)

        def face(t, before):
            def at(n, s):
                here = terms[n, t + 1]
                if s < 2:
                    return shifted(terms[n, t], here, None, s - 2, lane)
                return shifted(None, here, terms[n, t + 2] if s > 2 else None, s - 2, lane)

            flux = face_terms(
                [[at(c, s) for c in range(5)] for s in range(5)],
                [[at(5 + c, s) for c in range(5)] for s in range(5)],
                [at(10 + c, 2) for c in range(5)],
                [at(15 + c, 2) for c in range(5)],
                at(20, 2),
            )
            start = pl.multiple_of(t * lanes, lanes)
            row = pl.multiple_of(t * bands, bands)
            for c, now, old in zip(theta_order, flux, before):
                change = now - shifted(old, now, None, -1, lane)
                other = rows[c, pl.ds(p, batch), pl.ds(row, bands)]
                acc[c, pl.ds(p + 1, batch), :, pl.ds(start, lanes)] = change + other
            return flux

        lax.fori_loop(0, tiles, face, tuple(side[n, pl.ds(p, batch)] for n in range(5)))
        return carry

    lax.fori_loop(0, planes // batch, pair, 0)


def axial_faces(get, count, first, acc, terms, width):
    step = batch * lanes

    def columns(g, carry):
        start = pl.multiple_of(g * step, step)

        def cell(i):
            return with_terms([get(c, i, start) for c in axial_order])

        def interface(i, left):
            right = cell(i + 1)
            for n, value in enumerate(interface_terms(left, right)):
                for b in range(batch):
                    terms[n, i, b] = value[:, b * lanes : (b + 1) * lanes]
            return right

        lax.fori_loop(0, count + 4, interface, cell(0))

        def face(i, carry):
            flux = face_at(terms, i)
            for c, value in zip(axial_order, flux):
                for b in range(batch):
                    place = pl.ds(pl.multiple_of(start + b * lanes, lanes), lanes)
                    acc[c, first + i, :, place] += value[b]
                    acc[c, first + i + 1, :, place] -= value[b]
            return carry

        lax.fori_loop(0, count, face, 0)
        return carry

    lax.fori_loop(0, width // step, columns, 0)


def axial_inner(ids, section, acc, terms):
    planes, bands, width = section.shape[1:]
    first = jnp.where(ids[0] == 0, 0, ghosts)
    for c in range(5):
        acc[c, 0] = jnp.zeros((bands, width), jnp.float32)
        acc[c, planes + 1] = jnp.zeros((bands, width), jnp.float32)

    def get(c, i, start):
        plane = jnp.clip(first + i - ghosts, 0, planes - 1)
        return section[c, plane, :, pl.ds(start, batch * lanes)]

    axial_faces(get, planes + 1 - ghosts, first, acc, terms, width)


def main(ids, section, own_low, left_high, right_low, low_radial, high_radial):
    _, planes, bands, width = section.shape
    tiles = width // lanes
    depth = max(bands + 2 * ghosts, tiles + 2, planes + 2 * ghosts)
    vmem = pl.BlockSpec(memory_space=pltpu.VMEM)
    faces = (planes + 1) * tiles + planes * (tiles + bands + 1)
    return pl.pallas_call(
        main_kernel,
        in_specs=[pl.BlockSpec(memory_space=pltpu.SMEM)] + [vmem] * 6,
        out_shape=jax.ShapeDtypeStruct((5, planes + 2, bands, width), jnp.float32),
        scratch_shapes=[
            pltpu.VMEM((5, planes, bands * tiles, lanes), jnp.float32),
            pltpu.VMEM((5, bands + 2 * ghosts, planes, tiles, lanes), jnp.float32),
            pltpu.VMEM((21, depth, batch, 8, lanes), jnp.float32),
            pltpu.VMEM((5, planes, bands, lanes), jnp.float32),
            pltpu.VMEM((5, 2, planes, bands, lanes), jnp.float32),
        ],
        compiler_params=pltpu.CompilerParams(vmem_limit_bytes=vmem_bytes),
        cost_estimate=pl.CostEstimate(
            flops=faces * 8 * lanes * 700, bytes_accessed=section.size * 16, transcendentals=faces * 8 * lanes * 30
        ),
        name="inner",
    )(ids, section, own_low, left_high, right_low, low_radial, high_radial)


def tail_kernel(ids, section, base, acc, ghost, out, padded, total, terms):
    planes, bands, width = section.shape[1:]
    front = ids[0] == 0
    kept = planes - 1
    own = jnp.where(front, 1, 0)
    own_at = jnp.where(front, 0, ghosts)
    ghost_at = jnp.where(front, kept, 0)
    first = jnp.where(front, planes + 1 - ghosts, 0)
    for c in range(5):

        def copy_plane(i, carry):
            padded[c, own_at + i] = section[c, own + i]
            return carry

        lax.fori_loop(0, kept, copy_plane, 0)

        def copy_ghost(i, carry):
            padded[c, ghost_at + i] = ghost[c, i]
            return carry

        lax.fori_loop(0, ghosts, copy_ghost, 0)

        def copy_total(i, carry):
            total[c, i] = acc[c, i]
            return carry

        lax.fori_loop(0, planes + 2, copy_total, 0)

    def get(c, i, start):
        return padded[c, i, :, pl.ds(start, batch * lanes)]

    axial_faces(get, ghosts, first, total, terms, width)
    for c in range(5):

        def update(p, carry):
            change = (-0.25 * step_ratio / flux_scale) * total[c, p + 1]
            out[c, p] = 0.75 * base[c, p] + (0.25 * section[c, p] + change)
            return carry

        lax.fori_loop(0, planes, update, 0)


def tail(ids, section, base, acc, ghost):
    _, planes, bands, width = section.shape
    vmem = pl.BlockSpec(memory_space=pltpu.VMEM)
    return pl.pallas_call(
        tail_kernel,
        in_specs=[pl.BlockSpec(memory_space=pltpu.SMEM)] + [vmem] * 4,
        out_shape=jax.ShapeDtypeStruct(section.shape, jnp.float32),
        scratch_shapes=[
            pltpu.VMEM((5, planes - 1 + ghosts, bands, width), jnp.float32),
            pltpu.VMEM((5, planes + 2, bands, width), jnp.float32),
            pltpu.VMEM((21, 2 * ghosts + 1, batch, 8, lanes), jnp.float32),
        ],
        compiler_params=pltpu.CompilerParams(vmem_limit_bytes=vmem_bytes),
        name="tail",
    )(ids, section, base, acc, ghost)


def mortar_ghost(section, rotor_step, block_index):
    width = section.shape[3]
    offset = rotor_step[0] // 4
    fraction = (rotor_step[0] % 4).astype(jnp.float32) / 4.0
    outgoing = jnp.where(block_index == 0, section[:, -ghosts:], section[:, :ghosts])
    slab_count = lax.axis_size("theta")
    slab_index = lax.axis_index("theta")
    turns = offset // width
    facing = lax.ppermute(outgoing, "blk", [(0, 1), (1, 0)])
    whole = lax.all_gather(facing, "theta", axis=3, tiled=True)
    doubled = jnp.concatenate([whole, whole], axis=3)
    start = (turns - 1 - slab_index) % slab_count * width
    window = lax.dynamic_slice_in_dim(doubled, start, 2 * width, 3)
    reversed_window = window[..., ::-1]
    remainder = offset % width
    low_part = lax.dynamic_slice_in_dim(reversed_window, width - remainder, width, 3)
    high_part = lax.dynamic_slice_in_dim(reversed_window, width - remainder - 1, width, 3)
    ghost = (1.0 - fraction) * low_part + fraction * high_part
    return jnp.concatenate([ghost[:2], -ghost[2:3], ghost[3:]], axis=0)


def shards(base_state, section_state, rotor_step):
    block_index = lax.axis_index("blk")
    slab_count = lax.axis_size("theta")
    band_count = lax.axis_size("radial")
    ids = jnp.stack([block_index, lax.axis_index("radial"), band_count]).astype(jnp.int32)
    ghost = mortar_ghost(section_state, rotor_step, block_index)
    theta_low, theta_high, radial_low, radial_high = pack(section_state)
    up = [(i, (i + 1) % slab_count) for i in range(slab_count)]
    down = [((i + 1) % slab_count, i) for i in range(slab_count)]
    left_high = lax.ppermute(theta_high, "theta", up)
    right_low = lax.ppermute(theta_low, "theta", down)
    low_radial = lax.ppermute(radial_high, "radial", [(i, i + 1) for i in range(band_count - 1)])
    high_radial = lax.ppermute(radial_low, "radial", [(i + 1, i) for i in range(band_count - 1)])
    acc = main(ids, section_state, theta_low, left_high, right_low, low_radial, high_radial)
    return tail(ids, section_state, base_state, acc, ghost)


def solution(mesh):
    in_specs = (P(None, "blk", "radial", "theta"), P(None, "blk", "radial", "theta"), P())
    out_specs = P(None, "blk", "radial", "theta")
    return jax.shard_map(shards, mesh=mesh, in_specs=in_specs, out_specs=out_specs, check_vma=False)
```

time: 163 us -> 92.3 us (0.57)
  other arithmetic: 85.6 us -> 4.06 us
  Pallas kernels: 0 us -> 29.6 us
  local copies, waits for them, and re-layouts: 22.1 us -> 8.99 us
  waiting for transfers between devices: 27.8 us -> 22.1 us
    unnamed x12 -> x0, other arithmetic: 68.1 us -> none
    pallas_call x0 -> x3, Pallas kernels: none -> 29.6 us  [the longest x1 23.5 us: main(): pl.pallas_call(main_kernel, in_specs=[pl.BlockSpec(memory_space=pltpu.SME...]
    all_gather x1, waiting for transfers between devices: 27.8 us -> 8.06 us  [mortar_ghost(): whole = lax.all_gather(facing, 'theta', axis=3, tiled=True)]
    ppermute x5, waiting for transfers between devices: 0.01 us -> 14 us  [the longest x1 10.9 us: mortar_ghost(): facing = lax.ppermute(outgoing, 'blk', [(0, 1), (1, 0)])]
    slice x10 -> x1, local copies, waits for them, and re-layouts: 8.18 us -> 0.03 us  [mortar_ghost(): return jnp.concatenate([ghost[:2], -ghost[2:3], ghost[3:]], axis=0)]
    rev x1, local copies, waits for them, and re-layouts: 1.48 us -> 7.41 us  [mortar_ghost(): reversed_window = window[..., ::-1]]
    mul x9 -> x0, other arithmetic: 5.25 us -> none  [the longest x6 3.87 us: euler_flux(): flux = state * velocity[None]]
    unnamed x97 -> x6, local copies, waits for them, and re-layouts: 6.38 us -> 1.55 us
  transfers between devices with their start and end apart: 6 -> 6, of which waited for: 1 -> 4; matrix products, arithmetic and copies ran while one was open for 44% -> 0% of each run, Pallas kernels for 0% -> 26%
where the time goes in v1:
time: 92.3 us; the launch traced here: 90.9 us
  Pallas kernels  29.6 us (32%)
  waiting for transfers between devices  22.1 us (24%)
  between operations  14.2 us (15%)
  starting transfers between devices  12 us (13%)
  local copies, waits for them, and re-layouts  8.99 us (10%)
  other arithmetic  4.06 us (4%)
    pallas_call x1, Pallas kernels, main(): pl.pallas_call(main_kernel, in_specs=[pl.BlockSpec(memory_space=pltpu.SME...  23.5 us
    ppermute x1, waiting for transfers between devices, mortar_ghost(): facing = lax.ppermute(outgoing, 'blk', [(0, 1), (1, 0)])  10.9 us
    all_gather x1, waiting for transfers between devices, mortar_ghost(): whole = lax.all_gather(facing, 'theta', axis=3, tiled=True)  8.06 us
    rev x1, local copies, waits for them, and re-layouts, mortar_ghost(): reversed_window = window[..., ::-1]  7.41 us
    pallas_call x1, Pallas kernels, tail(): pl.pallas_call(tail_kernel, in_specs=[pl.BlockSpec(memory_space=pltpu.SME...  5.68 us
    ppermute x1, starting transfers between devices, shards(): lax.ppermute(radial_high, 'radial', [(i, i + 1) for i in range(band_count...  4.51 us
    ppermute x1, waiting for transfers between devices, shards(): lax.ppermute(radial_low, 'radial', [(i + 1, i) for i in range(band_count...  2.68 us
    concatenate x1, other arithmetic, mortar_ghost(): doubled = jnp.concatenate([whole, whole], axis=3)  2.29 us
  transfers between devices with their start and end apart: 6, of which 4 were waited for; matrix products, arithmetic and copies ran while one was open for 0% of the time, Pallas kernels for 26%

profile of v1, /device:TPU:1, one launch (start us, length us, event | category | flops | bytes accessed | tf_op | source)
XLA Modules:
  0.0 90.9 jit_solution(3226418003564337631)
XLA Ops:
  6.5 0.0 copy-start
  6.5 0.0 all-gather.2.cloned.1.call-start
  6.5 1.3 %slice_select_fusion = f32[5,3,8,1024]{3,2,1,0:T(8,128)S(1)} fusion(f32[5,6,8,1024]{3,2,1,0:T(8,128)} %section.5, pred[]{:T(512)S(6)} %eq.7), kind=kLoop, calls=%fused_computation.5 | loop fusion | flops 122880 | bytes 1474561 | tf_op jit(solution)/shard_map/jit(_where)/select_n | solution.py:469
  7.9 2.1 %collective-permute-start.4 = (f32[5,3,8,1024]{3,2,1,0:T(8,128)S(1)}, f32[5,3,8,1024]{3,2,1,0:T(8,128)S(1)}, u32[]{:S(2)}, u32[]{:S(2)}) collective-permute-start(f32[5,3,8,1024]{3,2,1,0:T(8,128)S(1)} %slice_select_fusion), channel_id=1, source_target_pairs={{0,16},{16,0},{1,17},{17,1},{2,18},{18,2},{3,19},{19,3},{4,20},{20... | collective-permute-start | bytes 1474568 | tf_op jit(solution)/shard_map/ppermute | solution.py:473
  10.0 10.9 %collective-permute-done.4 = f32[5,3,8,1024]{3,2,1,0:T(8,128)S(1)} collective-permute-done((f32[5,3,8,1024]{3,2,1,0:T(8,128)S(1)}, f32[5,3,8,1024]{3,2,1,0:T(8,128)S(1)}, u32[]{:S(2)}, u32[]{:S(2)}) %collective-permute-start.4) | collective-permute-done | bytes 491552 | tf_op jit(solution)/shard_map/ppermute | solution.py:473
  20.9 0.0 copy-start.2
  20.9 0.8 copy-done.2
  21.7 0.0 all-gather.2.cloned.1.call-update
  21.7 0.0 copy-done
  21.7 0.5 pack.1
  22.2 4.5 %collective-permute-start.2 = (f32[5,6,3,8,128]{4,3,2,1,0:T(8,128)S(1)}, f32[5,6,3,8,128]{4,3,2,1,0:T(8,128)S(1)}, u32[]{:S(2)}, u32[]{:S(2)}) collective-permute-start(f32[5,6,3,8,128]{4,3,2,1,0:T(8,128)S(1)} %get-tuple-element.11), channel_id=1, source_target_pairs={{0,1},{1,2},{2,3},{4,5},{5,6},{6,7},{8,9},{9,10},{10,11},{12,13},{... | collective-permute-start | bytes 1105928 | tf_op jit(solution)/shard_map/ppermute | solution.py:497
  26.7 1.9 %collective-permute-start.3 = (f32[5,6,3,8,128]{4,3,2,1,0:T(8,128)S(1)}, f32[5,6,3,8,128]{4,3,2,1,0:T(8,128)S(1)}, u32[]{:S(2)}, u32[]{:S(2)}) collective-permute-start(f32[5,6,3,8,128]{4,3,2,1,0:T(8,128)S(1)} %get-tuple-element.12), channel_id=1, source_target_pairs={{1,0},{2,1},{3,2},{5,4},{6,5},{7,6},{9,8},{10,9},{11,10},{13,12},{... | collective-permute-start | bytes 1105928 | tf_op jit(solution)/shard_map/ppermute | solution.py:498
  28.7 1.3 %collective-permute-start = (f32[5,8,128]{2,1,0:T(8,128)S(1)}, f32[5,8,128]{2,1,0:T(8,128)S(1)}, u32[]{:S(2)}, u32[]{:S(2)}) collective-permute-start(f32[5,8,128]{2,1,0:T(8,128)S(1)} %get-tuple-element.10), channel_id=1, source_target_pairs={{0,4},{4,8},{8,12},{12,0},{1,5},{5,9},{9,13},{13,1},{2,6},{6,10},{... | collective-permute-start | bytes 61448 | tf_op jit(solution)/shard_map/ppermute | solution.py:495
  30.0 2.1 %collective-permute-start.1 = (f32[5,8,128]{2,1,0:T(8,128)S(1)}, f32[5,8,128]{2,1,0:T(8,128)S(1)}, u32[]{:S(2)}, u32[]{:S(2)}) collective-permute-start(f32[5,8,128]{2,1,0:T(8,128)S(1)} %get-tuple-element.9.own_low), channel_id=1, source_target_pairs={{4,0},{8,4},{12,8},{0,12},{5,1},{9,5},{13,9},{1,13},{6,2},{10,6},{... | collective-permute-start | bytes 61448 | tf_op jit(solution)/shard_map/ppermute | solution.py:496
  32.1 0.1 pad_add_fusion.ids
  32.9 0.4 collective-permute-done.left_high
  33.3 0.0 collective-permute-done.1.right_low
  33.3 0.0 collective-permute-done.2.low_radial
  33.3 2.7 %collective-permute-done.3.high_radial = f32[5,6,3,8,128]{4,3,2,1,0:T(8,128)S(1)} collective-permute-done((f32[5,6,3,8,128]{4,3,2,1,0:T(8,128)S(1)}, f32[5,6,3,8,128]{4,3,2,1,0:T(8,128)S(1)}, u32[]{:S(2)}, u32[]{:S(2)}) %collective-permute-start.3) | collective-permute-done | bytes 368672 | tf_op jit(solution)/shard_map/ppermute | solution.py:498
  36.0 23.5 %inner.1.acc = f32[5,8,8,1024]{3,2,1,0:T(8,128)S(1)} custom-call(s32[3]{0:T(128)S(1)} %pad_add_fusion.ids, f32[5,6,8,1024]{3,2,1,0:T(8,128)S(1)} %copy-done, f32[5,8,128]{2,1,0:T(8,128)S(1)} %get-tuple-element.9.own_low, f32[5,8,128]{2,1,0:T(8,128)S(1)} %collective-permute-done.left_high, f32[5,8,128]{2,1,0:T(8,128)S(1)} %collective-permute-done.1.right_low, ...), custom_call_target="tpu_custom_call" | custom-call | flops 113254400 | bytes 3932160 | tf_op jit(solution)/shard_map/inner/pallas_call | solution.py:387
  59.5 8.1 %all-gather.2.cloned.1.call-done = f32[5,3,8,4096]{3,2,1,0:T(8,128)} async-done(((f32[5,3,8,1024]{3,2,1,0:T(8,128)}), f32[5,3,8,4096]{3,2,1,0:T(8,128)}) %all-gather.2.cloned.1.call-update) | async-done | bytes 1966096 | tf_op jit(solution)/shard_map/all_gather | solution.py:474
  67.5 2.3 %fusion = f32[5,3,8,2048]{3,2,1,0:T(8,128)} fusion(s32[]{:T(128)S(6)} %select_n.45, f32[5,3,8,4096]{3,2,1,0:T(8,128)} %all-gather.2.cloned.1.call-done), kind=kLoop, calls=%fused_computation.2 | loop fusion | flops 245760 | bytes 2949124 | tf_op jit(solution)/shard_map/concatenate | solution.py:475
  69.8 7.4 %rev.3 = f32[5,3,8,2048]{3,2,1,0:T(8,128)S(1)} reverse(f32[5,3,8,2048]{3,2,1,0:T(8,128)} %fusion), dimensions={3} | reverse | bytes 1966080 | tf_op jit(solution)/shard_map/rev | solution.py:478
  77.2 0.0 copy-start.1
  77.2 0.3 multiply_add_fusion
  77.7 0.8 copy-done.1
  78.4 5.7 %tail.1 = f32[5,6,8,1024]{3,2,1,0:T(8,128)} custom-call(s32[3]{0:T(128)S(1)} %pad_add_fusion.ids, f32[5,6,8,1024]{3,2,1,0:T(8,128)S(1)} %copy-done, f32[5,6,8,1024]{3,2,1,0:T(8,128)S(1)} %copy-done.1, f32[5,8,8,1024]{3,2,1,0:T(8,128)S(1)} %inner.1.acc, f32[5,3,8,1024]{3,2,1,0:T(8,128)S(1)} %pad_maximum_fusion.ghost), custom_call_target="tpu_custom_call" | custom-call | tf_op jit(solution)/shard_map/tail/pallas_call | solution.py:451
  (3 shorter events, 0.1 us)
Async XLA Ops:
  6.5 15.2 %copy-start = (f32[5,6,8,1024]{3,2,1,0:T(8,128)S(1)}, f32[5,6,8,1024]{3,2,1,0:T(8,128)}, u32[]{:S(2)}) copy-start(f32[5,6,8,1024]{3,2,1,0:T(8,128)} %section.5) | copy-start | bytes 2949124
  6.5 61.0 %all-gather.2.cloned.1.call-start = ((), (), s32[]{:S(2)}) async-start(), calls=%async_computation | async-start | bytes 2457600 | tf_op jit(solution)/shard_map/all_gather | solution.py:474
  7.9 13.1 %collective-permute-start.4 = (f32[5,3,8,1024]{3,2,1,0:T(8,128)S(1)}, f32[5,3,8,1024]{3,2,1,0:T(8,128)S(1)}, u32[]{:S(2)}, u32[]{:S(2)}) collective-permute-start(f32[5,3,8,1024]{3,2,1,0:T(8,128)S(1)} %slice_select_fusion), channel_id=1, source_target_pairs={{0,16},{16,0},{1,17},{17,1},{2,18},{18,2},{3,19},{19,3},{4,20},{20... | collective-permute-start | bytes 1474568 | tf_op jit(solution)/shard_map/ppermute | solution.py:473
  20.9 0.8 copy-start.2
  22.2 11.1 %collective-permute-start.2 = (f32[5,6,3,8,128]{4,3,2,1,0:T(8,128)S(1)}, f32[5,6,3,8,128]{4,3,2,1,0:T(8,128)S(1)}, u32[]{:S(2)}, u32[]{:S(2)}) collective-permute-start(f32[5,6,3,8,128]{4,3,2,1,0:T(8,128)S(1)} %get-tuple-element.11), channel_id=1, source_target_pairs={{0,1},{1,2},{2,3},{4,5},{5,6},{6,7},{8,9},{9,10},{10,11},{12,13},{... | collective-permute-start | bytes 1105928 | tf_op jit(solution)/shard_map/ppermute | solution.py:497
  26.7 9.2 %collective-permute-start.3 = (f32[5,6,3,8,128]{4,3,2,1,0:T(8,128)S(1)}, f32[5,6,3,8,128]{4,3,2,1,0:T(8,128)S(1)}, u32[]{:S(2)}, u32[]{:S(2)}) collective-permute-start(f32[5,6,3,8,128]{4,3,2,1,0:T(8,128)S(1)} %get-tuple-element.12), channel_id=1, source_target_pairs={{1,0},{2,1},{3,2},{5,4},{6,5},{7,6},{9,8},{10,9},{11,10},{13,12},{... | collective-permute-start | bytes 1105928 | tf_op jit(solution)/shard_map/ppermute | solution.py:498
  28.7 4.6 %collective-permute-start = (f32[5,8,128]{2,1,0:T(8,128)S(1)}, f32[5,8,128]{2,1,0:T(8,128)S(1)}, u32[]{:S(2)}, u32[]{:S(2)}) collective-permute-start(f32[5,8,128]{2,1,0:T(8,128)S(1)} %get-tuple-element.10), channel_id=1, source_target_pairs={{0,4},{4,8},{8,12},{12,0},{1,5},{5,9},{9,13},{13,1},{2,6},{6,10},{... | collective-permute-start | bytes 61448 | tf_op jit(solution)/shard_map/ppermute | solution.py:495
  30.0 3.3 %collective-permute-start.1 = (f32[5,8,128]{2,1,0:T(8,128)S(1)}, f32[5,8,128]{2,1,0:T(8,128)S(1)}, u32[]{:S(2)}, u32[]{:S(2)}) collective-permute-start(f32[5,8,128]{2,1,0:T(8,128)S(1)} %get-tuple-element.9.own_low), channel_id=1, source_target_pairs={{4,0},{8,4},{12,8},{0,12},{5,1},{9,5},{13,9},{1,13},{6,2},{10,6},{... | collective-permute-start | bytes 61448 | tf_op jit(solution)/shard_map/ppermute | solution.py:496
  77.2 1.2 %copy-start.1 = (f32[5,6,8,1024]{3,2,1,0:T(8,128)S(1)}, f32[5,6,8,1024]{3,2,1,0:T(8,128)}, u32[]{:S(2)}) copy-start(f32[5,6,8,1024]{3,2,1,0:T(8,128)} %base.1) | copy-start | bytes 2949124
Sparse Core Ops, SparseCore 0:
  21.8 45.6 all-gather.1
